TPU v7x, 512 devices: a whole 4x8x8 slice. The times are simulated.
512 devices in a mesh: gx: 32 (over z_hi, y, core), gy: 16 (over z_lo, x).
Axes of the slice: x: 4, y: 8, z: 8 (z_hi: 2, z_lo: 4; z = z_hi * 4 + z_lo), core: 2. Of those that a mesh axis runs over, the one named last changes fastest.
Arguments:
- offsets: bfloat16 [642, 3, 65536], P(None, None, ('gx', 'gy')), may hold values from -6 to 6
- metric: bfloat16 [642, 65536], P(None, ('gx', 'gy')), may hold values from 0.29882812 to 3
- centers: float32 [3, 65536], P(None, ('gx', 'gy')), may hold values from -6 to 6
- lap_matrix: bfloat16 [642, 642], replicated, may hold values from -0.25 to 0.25
- bend_matrix: bfloat16 [642, 642], replicated, may hold values from -0.25 to 0.25
- mig_slots: int32 [512, 8, 4], P(('gx', 'gy')), may hold values from 0 to 127, as said below
- contact_ids: int32 [512, 8, 4], P(('gx', 'gy')), may hold values from 0 to 767
- contact_local: int32 [512, 8, 4], P(('gx', 'gy')), may hold values from 0 to 127
- contact_count: int32 [512, 8], P(('gx', 'gy')), may hold values from 1 to 4, as said below
Outputs:
- new_offsets: bfloat16 [642, 3, 65536], P(None, None, ('gx', 'gy'))
- new_metric: bfloat16 [642, 65536], P(None, ('gx', 'gy'))
- new_centers: float32 [3, 65536], P(None, ('gx', 'gy'))
Inputs may be any that keep to these rules, and one draw needn't show every extreme that they name: `mig_slots`: within one tile the slots named over all 8 directions are distinct. `contact_count`: in every draw some tile has exactly 4 live entries toward some neighbour. `contact_ids`: entries at or past the count are unused.
All inputs are finite; a program needn't handle non-finite values.
Results may differ from a plain program's by a relative error of at most 0.0032.
Values sent between devices are 32-bit elements; how exact they have to be, the bound alone decides.
A program may use at most 64 MiB of HBM per device.

v0:
```python
import jax
import jax.numpy as jnp
from jax import lax
from jax.sharding import PartitionSpec as P

V = 642
NBLK = 6
VB = 107
GRP = 2


DIRECTIONS = ((-1, -1), (-1, 0), (-1, 1), (0, -1), (0, 1), (1, -1), (1, 0), (1, 1))
TENSION = 0.5
GAUSS_WIDTH = 4.0
STRENGTH = 8.0
TIME_STEP = 0.25


def from_behind(array, axis, by):
    size = lax.axis_size(axis)
    return lax.ppermute(array, axis, [(i, (i + by) % size) for i in range(size)])


def membrane(offset_part, metric_part, lap_matrix, bend_matrix):
    cell_count = offset_part.shape[2]
    flattened = offset_part.reshape(V, 3 * cell_count)
    curvature = jnp.dot(lap_matrix, flattened, preferred_element_type=jnp.float32).reshape(
        V, 3, cell_count
    )
    metric_col = metric_part.astype(jnp.float32)[:, None, :]
    weighted = (metric_col * curvature).astype(jnp.bfloat16)
    bending = jnp.dot(
        lap_matrix, weighted.reshape(V, 3 * cell_count), preferred_element_type=jnp.float32
    ).reshape(V, 3, cell_count)
    shear_term = jnp.dot(bend_matrix, flattened, preferred_element_type=jnp.float32).reshape(
        V, 3, cell_count
    )
    return metric_col * (TENSION * curvature - bending) - shear_term


def pair_forces(near_rows, far_rows):
    highest = lax.Precision.HIGHEST
    near_sq = jnp.sum(near_rows * near_rows, axis=1)
    far_sq = jnp.sum(far_rows * far_rows, axis=1)
    cross = jnp.einsum("gca,gcv->gav", near_rows, far_rows, precision=highest)
    kernel = jnp.exp(-(near_sq[:, :, None] + far_sq[:, None, :] - 2.0 * cross) / GAUSS_WIDTH)
    row_total = jnp.sum(kernel, axis=2)
    col_total = jnp.sum(kernel, axis=1)
    factor = STRENGTH / VB
    on_near = factor * (
        near_rows * row_total[:, None, :]
        - jnp.einsum("gav,gcv->gca", kernel, far_rows, precision=highest)
    )
    on_far = -factor * (
        jnp.einsum("gav,gca->gcv", kernel, near_rows, precision=highest)
        - far_rows * col_total[:, None, :]
    )
    return (on_near, on_far)


def to_neighbours(bundles, direction_sign):
    result = []
    for heading in range(8):
        step_x, step_y = DIRECTIONS[heading]
        bundle = bundles[heading]
        if step_x != 0:
            bundle = from_behind((bundle[0], bundle[1]), "gx", direction_sign * step_x)
        if step_y != 0:
            bundle = from_behind((bundle[0], bundle[1]), "gy", direction_sign * step_y)
        result.append(bundle)
    return result


def partner_work(rows_in, active_in, partner):
    live_count = jnp.sum(active_in).astype(jnp.int32)
    group_total = (live_count + GRP - 1) // GRP

    def one_group(group_index, state_pair):
        returned, far_force = state_pair
        first_row = group_index * GRP
        near_rows = lax.dynamic_slice_in_dim(rows_in, first_row, GRP, 0)
        far_rows = lax.dynamic_slice_in_dim(partner, first_row, GRP, 0)
        weights_live = lax.dynamic_slice_in_dim(active_in, first_row, GRP, 0)[:, None, None]
        on_near, on_far = pair_forces(near_rows, far_rows)
        returned = lax.dynamic_update_slice_in_dim(returned, on_near * weights_live, first_row, 0)
        far_force = lax.dynamic_update_slice_in_dim(far_force, on_far * weights_live, first_row, 0)
        return (returned, far_force)

    initial = (jnp.zeros(rows_in.shape, jnp.float32), jnp.zeros(partner.shape, jnp.float32))
    return lax.fori_loop(0, group_total, one_group, initial)


def per_device(
    offsets,
    metric,
    centers,
    lap_matrix,
    bend_matrix,
    mig_slots,
    contact_ids,
    contact_local,
    contact_count,
):
    cell_count = offsets.shape[2]
    position = centers[None, :, :] + offsets.astype(jnp.float32)
    cell_major = jnp.transpose(position, (2, 1, 0))
    entry_ids = contact_ids[0]
    owner_cell = entry_ids // NBLK
    owner_block = entry_ids % NBLK
    capacity = entry_ids.shape[1]
    blocked = cell_major.reshape(cell_count, 3, NBLK, VB)
    block_rows = blocked[owner_cell, :, owner_block, :]
    active = (jnp.arange(capacity)[None, :] < contact_count[0][:, None]).astype(jnp.float32)
    arrived = to_neighbours([(block_rows[heading], active[heading]) for heading in range(8)], 1)
    answers = []
    far_parts = []
    slot_parts = []
    for heading in range(8):
        rows_in, active_in = arrived[heading]
        target_slots = contact_local[0, heading]
        partner = cell_major[target_slots]
        returned, far_force = partner_work(rows_in, active_in, partner)
        far_parts.append(far_force)
        slot_parts.append(target_slots)
        answers.append((returned, active_in))
    far_stack = jnp.concatenate(far_parts, axis=0)
    slot_stack = jnp.concatenate(slot_parts, axis=0)
    contact_major = jnp.zeros((cell_count, 3, V), jnp.float32)
    contact_major = contact_major.at[slot_stack].add(far_stack)
    replies = to_neighbours(answers, -1)
    near_stack = jnp.concatenate(
        [replies[heading][0] * replies[heading][1][:, None, None] for heading in range(8)], axis=0
    )
    gridded = contact_major.reshape(cell_count, 3, NBLK, VB)
    gridded = gridded.at[owner_cell.reshape(-1), :, owner_block.reshape(-1), :].add(near_stack)
    contact = jnp.transpose(gridded.reshape(cell_count, 3, V), (2, 1, 0))
    membrane_force = membrane(offsets, metric, lap_matrix, bend_matrix)
    displaced = position + TIME_STEP * (membrane_force + contact)
    displaced_major = jnp.transpose(displaced, (2, 1, 0))
    metric_major = jnp.transpose(metric.astype(jnp.float32), (1, 0))
    slot_table = mig_slots[0]
    bundles = [
        (displaced_major[slot_table[heading]], metric_major[slot_table[heading]])
        for heading in range(8)
    ]
    incoming = to_neighbours(bundles, 1)
    flat_slots = slot_table.reshape(-1)
    arriving = jnp.concatenate([incoming[heading][0] for heading in range(8)], axis=0)
    arriving_metric = jnp.concatenate([incoming[heading][1] for heading in range(8)], axis=0)
    settled_major = displaced_major.at[flat_slots].set(arriving)
    metric_settled = metric_major.at[flat_slots].set(arriving_metric)
    centre_major = jnp.mean(settled_major, axis=2)
    new_offsets = jnp.transpose(
        (settled_major - centre_major[:, :, None]).astype(jnp.bfloat16), (2, 1, 0)
    )
    new_metric = jnp.transpose(metric_settled.astype(jnp.bfloat16), (1, 0))
    new_centers = jnp.transpose(centre_major, (1, 0))
    return (new_offsets, new_metric, new_centers)


def solution(mesh):
    return jax.shard_map(
        per_device,
        mesh=mesh,
        in_specs=(
            P(None, None, ("gx", "gy")),
            P(None, ("gx", "gy")),
            P(None, ("gx", "gy")),
            P(),
            P(),
            P(("gx", "gy"), None, None),
            P(("gx", "gy"), None, None),
            P(("gx", "gy"), None, None),
            P(("gx", "gy"), None),
        ),
        out_specs=(P(None, None, ("gx", "gy")), P(None, ("gx", "gy")), P(None, ("gx", "gy"))),
        check_vma=False,
    )
```

profile of v0, /device:TPU:1, one launch (start us, length us, event | category | flops | bytes accessed | tf_op | source)
XLA Modules:
  0.0 476.7 jit_solution(14684587192260922128)
XLA Ops:
  2.1 8.8 %collective-permute-start = (f32[4]{0:T(128)}, f32[4]{0:T(128)}, u32[]{:S(2)}, u32[]{:S(2)}) collective-permute-start(f32[4]{0:T(128)} %get-tuple-element.591), channel_id=1, source_target_pairs={{0,496},{16,0},{32,16},{48,32},{64,48},{80,64},{96,80},{112,96},{1... | collective-permute-start | bytes 56 | tf_op jit(solution)/shard_map/ppermute | solution.py:21
  18.5 7.9 %collective-permute-start.2 = (f32[4,3,107]{2,1,0:T(4,128)S(1)}, f32[4,3,107]{2,1,0:T(4,128)}, u32[]{:S(2)}, u32[]{:S(2)}) collective-permute-start(f32[4,3,107]{2,1,0:T(4,128)S(1)} %get-tuple-element.583), channel_id=1, source_target_pairs={{0,496},{16,0},{32,16},{48,32},{64,48},{80,64},{96,80},{112,96},{1... | collective-permute-start | bytes 15416 | tf_op jit(solution)/shard_map/ppermute | solution.py:21
  73.1 7.1 %collective-permute-start.10 = (f32[4]{0:T(128)S(1)}, f32[4]{0:T(128)S(1)}, u32[]{:S(2)}, u32[]{:S(2)}) collective-permute-start(f32[4]{0:T(128)S(1)} %get-tuple-element.588), channel_id=1, source_target_pairs={{0,15},{1,0},{2,1},{3,2},{4,3},{5,4},{6,5},{7,6},{8,7},{9,8},{10,9... | collective-permute-start | bytes 56 | tf_op jit(solution)/shard_map/ppermute | solution.py:21
  95.6 9.3 %collective-permute-start.8 = (f32[4,3,107]{2,1,0:T(4,128)S(1)}, f32[4,3,107]{2,1,0:T(4,128)S(1)}, u32[]{:S(2)}, u32[]{:S(2)}) collective-permute-start(f32[4,3,107]{2,1,0:T(4,128)S(1)} %get-tuple-element.581), channel_id=1, source_target_pairs={{0,496},{16,0},{32,16},{48,32},{64,48},{80,64},{96,80},{112,96},{1... | collective-permute-start | bytes 15416 | tf_op jit(solution)/shard_map/ppermute | solution.py:21
  117.7 5.2 %collective-permute-done.7 = f32[4]{0:T(128)S(1)} collective-permute-done((f32[4]{0:T(128)}, f32[4]{0:T(128)S(1)}, u32[]{:S(2)}, u32[]{:S(2)}) %collective-permute-start.7) | collective-permute-done | bytes 48 | tf_op jit(solution)/shard_map/ppermute | solution.py:21
  129.7 8.9 %collective-permute-done.20 = f32[4]{0:T(128)S(1)} collective-permute-done((f32[4]{0:T(128)S(1)}, f32[4]{0:T(128)S(1)}, u32[]{:S(2)}, u32[]{:S(2)}) %collective-permute-start.20) | collective-permute-done | bytes 48 | tf_op jit(solution)/shard_map/ppermute | solution.py:21
  170.2 15.6 %collective-permute-start.60 = (f32[4,642]{1,0:T(4,128)}, f32[4,642]{1,0:T(4,128)}, u32[]{:S(2)}, u32[]{:S(2)}) collective-permute-start(f32[4,642]{1,0:T(4,128)} %gather_fusion.17), channel_id=1, source_target_pairs={{0,496},{16,0},{32,16},{48,32},{64,48},{80,64},{96,80},{112,96},{1... | collective-permute-start | bytes 30824 | tf_op jit(solution)/shard_map/ppermute | solution.py:21
  185.8 7.5 %collective-permute-start.3 = (f32[4,3,107]{2,1,0:T(4,128)}, f32[4,3,107]{2,1,0:T(4,128)S(1)}, u32[]{:S(2)}, u32[]{:S(2)}) collective-permute-start(f32[4,3,107]{2,1,0:T(4,128)} %collective-permute-done.2), channel_id=1, source_target_pairs={{0,15},{1,0},{2,1},{3,2},{4,3},{5,4},{6,5},{7,6},{8,7},{9,8},{10,9... | collective-permute-start | bytes 15416 | tf_op jit(solution)/shard_map/ppermute | solution.py:21
  193.4 6.1 %while.102 = (s32[]{:T(128)}, f32[4,3,107]{2,1,0:T(4,128)S(1)}, f32[4,3,642]{2,1,0:T(4,128)S(1)}, s32[]{:T(128)}, f32[4,3,107]{2,1,0:T(4,128)S(1)}, /*index=5*/f...) while((s32[]{:T(128)}, f32[4,3,107]{2,1,0:T(4,128)S(1)}, ...), condition=%wide.region_48.49_spmd, body=%wide.region_43.48_spmd.sunk | while | flops 15819104 | bytes 2039927 | solution.py:90
  199.4 6.9 %collective-permute-start.63 = (f32[4,642]{1,0:T(4,128)}, f32[4,642]{1,0:T(4,128)}, u32[]{:S(2)}, u32[]{:S(2)}) collective-permute-start(f32[4,642]{1,0:T(4,128)} %gather_fusion.19), channel_id=1, source_target_pairs={{0,496},{16,0},{32,16},{48,32},{64,48},{80,64},{96,80},{112,96},{1... | collective-permute-start | bytes 30824 | tf_op jit(solution)/shard_map/ppermute | solution.py:21
  214.7 5.9 %collective-permute-start.17 = (f32[4,3,107]{2,1,0:T(4,128)S(1)}, f32[4,3,107]{2,1,0:T(4,128)S(1)}, u32[]{:S(2)}, u32[]{:S(2)}) collective-permute-start(f32[4,3,107]{2,1,0:T(4,128)S(1)} %collective-permute-done.16), channel_id=1, source_target_pairs={{0,15},{1,0},{2,1},{3,2},{4,3},{5,4},{6,5},{7,6},{8,7},{9,8},{10,9... | collective-permute-start | bytes 15416 | tf_op jit(solution)/shard_map/ppermute | solution.py:21
  231.5 6.3 %while.101 = (s32[]{:T(128)}, f32[4,3,107]{2,1,0:T(4,128)S(1)}, f32[4,3,642]{2,1,0:T(4,128)S(1)}, s32[]{:T(128)}, f32[4,3,107]{2,1,0:T(4,128)S(1)}, /*index=5*/f...) while((s32[]{:T(128)}, f32[4,3,107]{2,1,0:T(4,128)S(1)}, ...), condition=%wide.region_41.42_spmd, body=%wide.region_36.41_spmd.sunk | while | flops 15819104 | bytes 2039927 | solution.py:90
  269.8 7.5 %collective-permute-start.33 = (f32[4]{0:T(128)S(1)}, f32[4]{0:T(128)S(1)}, u32[]{:S(2)}, u32[]{:S(2)}) collective-permute-start(f32[4]{0:T(128)S(1)} %collective-permute-done.32), channel_id=1, source_target_pairs={{0,15},{1,0},{2,1},{3,2},{4,3},{5,4},{6,5},{7,6},{8,7},{9,8},{10,9... | collective-permute-start | bytes 56 | tf_op jit(solution)/shard_map/ppermute | solution.py:21
  287.6 7.3 %collective-permute-start.36 = (f32[4,3,107]{2,1,0:T(4,128)S(1)}, f32[4,3,107]{2,1,0:T(4,128)S(1)}, u32[]{:S(2)}, u32[]{:S(2)}) collective-permute-start(f32[4,3,107]{2,1,0:T(4,128)S(1)} %copy-done.23), channel_id=1, source_target_pairs={{0,15},{1,0},{2,1},{3,2},{4,3},{5,4},{6,5},{7,6},{8,7},{9,8},{10,9... | collective-permute-start | bytes 15416 | tf_op jit(solution)/shard_map/ppermute | solution.py:21
  294.9 12.3 %collective-permute-start.38 = (f32[4,3,107]{2,1,0:T(4,128)S(1)}, f32[4,3,107]{2,1,0:T(4,128)S(1)}, u32[]{:S(2)}, u32[]{:S(2)}) collective-permute-start(f32[4,3,107]{2,1,0:T(4,128)S(1)} %copy-done.27), channel_id=1, source_target_pairs={{0,496},{16,0},{32,16},{48,32},{64,48},{80,64},{96,80},{112,96},{1... | collective-permute-start | bytes 15416 | tf_op jit(solution)/shard_map/ppermute | solution.py:21
  322.8 10.7 %collective-permute-start.42 = (f32[4,3,107]{2,1,0:T(4,128)S(1)}, f32[4,3,107]{2,1,0:T(4,128)S(1)}, u32[]{:S(2)}, u32[]{:S(2)}) collective-permute-start(f32[4,3,107]{2,1,0:T(4,128)S(1)} %copy-done.25), channel_id=1, source_target_pairs={{0,496},{16,0},{32,16},{48,32},{64,48},{80,64},{96,80},{112,96},{1... | collective-permute-start | bytes 15416 | tf_op jit(solution)/shard_map/ppermute | solution.py:21
  360.3 6.0 %collective-permute-start.65 = (f32[4,642]{1,0:T(4,128)S(1)}, f32[4,642]{1,0:T(4,128)S(1)}, u32[]{:S(2)}, u32[]{:S(2)}) collective-permute-start(f32[4,642]{1,0:T(4,128)S(1)} %copy-done.13), channel_id=1, source_target_pairs={{0,15},{1,0},{2,1},{3,2},{4,3},{5,4},{6,5},{7,6},{8,7},{9,8},{10,9... | collective-permute-start | bytes 30824 | tf_op jit(solution)/shard_map/ppermute | solution.py:21
  377.3 7.5 %collective-permute-start.61 = (f32[4,642]{1,0:T(4,128)}, f32[4,642]{1,0:T(4,128)S(1)}, u32[]{:S(2)}, u32[]{:S(2)}) collective-permute-start(f32[4,642]{1,0:T(4,128)} %collective-permute-done.60), channel_id=1, source_target_pairs={{0,15},{1,0},{2,1},{3,2},{4,3},{5,4},{6,5},{7,6},{8,7},{9,8},{10,9... | collective-permute-start | bytes 30824 | tf_op jit(solution)/shard_map/ppermute | solution.py:21
  386.8 7.3 %collective-permute-start.68 = (f32[4,642]{1,0:T(4,128)}, f32[4,642]{1,0:T(4,128)S(1)}, u32[]{:S(2)}, u32[]{:S(2)}) collective-permute-start(f32[4,642]{1,0:T(4,128)} %collective-permute-done.67), channel_id=1, source_target_pairs={{0,15},{1,0},{2,1},{3,2},{4,3},{5,4},{6,5},{7,6},{8,7},{9,8},{10,9... | collective-permute-start | bytes 30824 | tf_op jit(solution)/shard_map/ppermute | solution.py:21
  396.1 9.2 %collective-permute-start.48 = (f32[4,3,642]{2,1,0:T(4,128)S(1)}, f32[4,3,642]{2,1,0:T(4,128)S(1)}, u32[]{:S(2)}, u32[]{:S(2)}) collective-permute-start(f32[4,3,642]{2,1,0:T(4,128)S(1)} %gather_fusion.9), channel_id=1, source_target_pairs={{0,496},{16,0},{32,16},{48,32},{64,48},{80,64},{96,80},{112,96},{1... | collective-permute-start | bytes 92456 | tf_op jit(solution)/shard_map/ppermute | solution.py:21
  412.6 8.8 %collective-permute-start.50 = (f32[4,3,642]{2,1,0:T(4,128)}, f32[4,3,642]{2,1,0:T(4,128)}, u32[]{:S(2)}, u32[]{:S(2)}) collective-permute-start(f32[4,3,642]{2,1,0:T(4,128)} %gather_fusion.10), channel_id=1, source_target_pairs={{0,496},{16,0},{32,16},{48,32},{64,48},{80,64},{96,80},{112,96},{1... | collective-permute-start | bytes 92456 | tf_op jit(solution)/shard_map/ppermute | solution.py:21
  423.4 7.3 %collective-permute-start.53 = (f32[4,3,642]{2,1,0:T(4,128)S(1)}, f32[4,3,642]{2,1,0:T(4,128)}, u32[]{:S(2)}, u32[]{:S(2)}) collective-permute-start(f32[4,3,642]{2,1,0:T(4,128)S(1)} %gather_fusion.12), channel_id=1, source_target_pairs={{0,15},{1,0},{2,1},{3,2},{4,3},{5,4},{6,5},{7,6},{8,7},{9,8},{10,9... | collective-permute-start | bytes 92456 | tf_op jit(solution)/shard_map/ppermute | solution.py:21
  434.3 7.3 %collective-permute-start.49 = (f32[4,3,642]{2,1,0:T(4,128)S(1)}, f32[4,3,642]{2,1,0:T(4,128)S(1)}, u32[]{:S(2)}, u32[]{:S(2)}) collective-permute-start(f32[4,3,642]{2,1,0:T(4,128)S(1)} %collective-permute-done.48), channel_id=1, source_target_pairs={{0,15},{1,0},{2,1},{3,2},{4,3},{5,4},{6,5},{7,6},{8,7},{9,8},{10,9... | collective-permute-start | bytes 92456 | tf_op jit(solution)/shard_map/ppermute | solution.py:21
  455.9 7.9 %collective-permute-start.56 = (f32[4,3,642]{2,1,0:T(4,128)S(1)}, f32[4,3,642]{2,1,0:T(4,128)S(1)}, u32[]{:S(2)}, u32[]{:S(2)}) collective-permute-start(f32[4,3,642]{2,1,0:T(4,128)S(1)} %collective-permute-done.55), channel_id=1, source_target_pairs={{0,15},{1,0},{2,1},{3,2},{4,3},{5,4},{6,5},{7,6},{8,7},{9,8},{10,9... | collective-permute-start | bytes 92456 | tf_op jit(solution)/shard_map/ppermute | solution.py:21
  (424 shorter events, 304.7 us)
Async XLA Ops:
  2.1 104.2 %collective-permute-start = (f32[4]{0:T(128)}, f32[4]{0:T(128)}, u32[]{:S(2)}, u32[]{:S(2)}) collective-permute-start(f32[4]{0:T(128)} %get-tuple-element.591), channel_id=1, source_target_pairs={{0,496},{16,0},{32,16},{48,32},{64,48},{80,64},{96,80},{112,96},{1... | collective-permute-start | bytes 56 | tf_op jit(solution)/shard_map/ppermute | solution.py:21
  18.5 151.7 %collective-permute-start.2 = (f32[4,3,107]{2,1,0:T(4,128)S(1)}, f32[4,3,107]{2,1,0:T(4,128)}, u32[]{:S(2)}, u32[]{:S(2)}) collective-permute-start(f32[4,3,107]{2,1,0:T(4,128)S(1)} %get-tuple-element.583), channel_id=1, source_target_pairs={{0,496},{16,0},{32,16},{48,32},{64,48},{80,64},{96,80},{112,96},{1... | collective-permute-start | bytes 15416 | tf_op jit(solution)/shard_map/ppermute | solution.py:21
  26.4 46.8 %collective-permute-start.4 = (f32[4]{0:T(128)}, f32[4]{0:T(128)S(1)}, u32[]{:S(2)}, u32[]{:S(2)}) collective-permute-start(f32[4]{0:T(128)} %get-tuple-element.590), channel_id=1, source_target_pairs={{0,496},{16,0},{32,16},{48,32},{64,48},{80,64},{96,80},{112,96},{1... | collective-permute-start | bytes 56 | tf_op jit(solution)/shard_map/ppermute | solution.py:21
  29.0 125.4 %collective-permute-start.5 = (f32[4,3,107]{2,1,0:T(4,128)}, f32[4,3,107]{2,1,0:T(4,128)S(1)}, u32[]{:S(2)}, u32[]{:S(2)}) collective-permute-start(f32[4,3,107]{2,1,0:T(4,128)} %get-tuple-element.582), channel_id=1, source_target_pairs={{0,496},{16,0},{32,16},{48,32},{64,48},{80,64},{96,80},{112,96},{1... | collective-permute-start | bytes 15416 | tf_op jit(solution)/shard_map/ppermute | solution.py:21
  31.7 78.3 %collective-permute-start.6 = (f32[4]{0:T(128)}, f32[4]{0:T(128)}, u32[]{:S(2)}, u32[]{:S(2)}) collective-permute-start(f32[4]{0:T(128)} %get-tuple-element.589), channel_id=1, source_target_pairs={{0,496},{16,0},{32,16},{48,32},{64,48},{80,64},{96,80},{112,96},{1... | collective-permute-start | bytes 56 | tf_op jit(solution)/shard_map/ppermute | solution.py:21
  95.6 103.8 %collective-permute-start.8 = (f32[4,3,107]{2,1,0:T(4,128)S(1)}, f32[4,3,107]{2,1,0:T(4,128)S(1)}, u32[]{:S(2)}, u32[]{:S(2)}) collective-permute-start(f32[4,3,107]{2,1,0:T(4,128)S(1)} %get-tuple-element.581), channel_id=1, source_target_pairs={{0,496},{16,0},{32,16},{48,32},{64,48},{80,64},{96,80},{112,96},{1... | collective-permute-start | bytes 15416 | tf_op jit(solution)/shard_map/ppermute | solution.py:21
  106.3 53.0 %collective-permute-start.11 = (f32[4,3,107]{2,1,0:T(4,128)}, f32[4,3,107]{2,1,0:T(4,128)S(1)}, u32[]{:S(2)}, u32[]{:S(2)}) collective-permute-start(f32[4,3,107]{2,1,0:T(4,128)} %get-tuple-element.580), channel_id=1, source_target_pairs={{0,15},{1,0},{2,1},{3,2},{4,3},{5,4},{6,5},{7,6},{8,7},{9,8},{10,9... | collective-permute-start | bytes 15416 | tf_op jit(solution)/shard_map/ppermute | solution.py:21
  154.4 57.0 %collective-permute-start.16 = (f32[4,3,107]{2,1,0:T(4,128)S(1)}, f32[4,3,107]{2,1,0:T(4,128)S(1)}, u32[]{:S(2)}, u32[]{:S(2)}) collective-permute-start(f32[4,3,107]{2,1,0:T(4,128)S(1)} %get-tuple-element.578), channel_id=1, source_target_pairs={{0,16},{16,32},{32,48},{48,64},{64,80},{80,96},{96,112},{112,128},... | collective-permute-start | bytes 15416 | tf_op jit(solution)/shard_map/ppermute | solution.py:21
  164.9 62.7 %collective-permute-start.22 = (f32[4,3,107]{2,1,0:T(4,128)S(1)}, f32[4,3,107]{2,1,0:T(4,128)S(1)}, u32[]{:S(2)}, u32[]{:S(2)}) collective-permute-start(f32[4,3,107]{2,1,0:T(4,128)S(1)} %get-tuple-element.576), channel_id=1, source_target_pairs={{0,16},{16,32},{32,48},{48,64},{64,80},{80,96},{96,112},{112,128},... | collective-permute-start | bytes 15416 | tf_op jit(solution)/shard_map/ppermute | solution.py:21
  170.2 190.1 %collective-permute-start.60 = (f32[4,642]{1,0:T(4,128)}, f32[4,642]{1,0:T(4,128)}, u32[]{:S(2)}, u32[]{:S(2)}) collective-permute-start(f32[4,642]{1,0:T(4,128)} %gather_fusion.17), channel_id=1, source_target_pairs={{0,496},{16,0},{32,16},{48,32},{64,48},{80,64},{96,80},{112,96},{1... | collective-permute-start | bytes 30824 | tf_op jit(solution)/shard_map/ppermute | solution.py:21
  199.4 166.8 %collective-permute-start.63 = (f32[4,642]{1,0:T(4,128)}, f32[4,642]{1,0:T(4,128)}, u32[]{:S(2)}, u32[]{:S(2)}) collective-permute-start(f32[4,642]{1,0:T(4,128)} %gather_fusion.19), channel_id=1, source_target_pairs={{0,496},{16,0},{32,16},{48,32},{64,48},{80,64},{96,80},{112,96},{1... | collective-permute-start | bytes 30824 | tf_op jit(solution)/shard_map/ppermute | solution.py:21
  224.8 39.1 %collective-permute-start.29 = (f32[4]{0:T(128)S(1)}, f32[4]{0:T(128)}, u32[]{:S(2)}, u32[]{:S(2)}) collective-permute-start(f32[4]{0:T(128)S(1)} %get-tuple-element.1327), channel_id=1, source_target_pairs={{0,16},{16,32},{32,48},{48,64},{64,80},{80,96},{96,112},{112,128},... | collective-permute-start | bytes 56 | tf_op jit(solution)/shard_map/ppermute | solution.py:21
  227.6 31.0 %collective-permute-start.27 = (f32[4]{0:T(128)S(1)}, f32[4]{0:T(128)S(1)}, u32[]{:S(2)}, u32[]{:S(2)}) collective-permute-start(f32[4]{0:T(128)S(1)} %collective-permute-done.26), channel_id=1, source_target_pairs={{0,1},{1,2},{2,3},{3,4},{4,5},{5,6},{6,7},{7,8},{8,9},{9,10},{10,1... | collective-permute-start | bytes 56 | tf_op jit(solution)/shard_map/ppermute | solution.py:21
  348.3 29.0 %collective-permute-start.70 = (f32[4,642]{1,0:T(4,128)}, f32[4,642]{1,0:T(4,128)}, u32[]{:S(2)}, u32[]{:S(2)}) collective-permute-start(f32[4,642]{1,0:T(4,128)} %gather_fusion.24), channel_id=1, source_target_pairs={{0,16},{16,32},{32,48},{48,64},{64,80},{80,96},{96,112},{112,128},... | collective-permute-start | bytes 30824 | tf_op jit(solution)/shard_map/ppermute | solution.py:21
  350.8 34.1 %collective-permute-start.62 = (f32[4,642]{1,0:T(4,128)}, f32[4,642]{1,0:T(4,128)S(1)}, u32[]{:S(2)}, u32[]{:S(2)}) collective-permute-start(f32[4,642]{1,0:T(4,128)} %gather_fusion.18), channel_id=1, source_target_pairs={{0,496},{16,0},{32,16},{48,32},{64,48},{80,64},{96,80},{112,96},{1... | collective-permute-start | bytes 30824 | tf_op jit(solution)/shard_map/ppermute | solution.py:21
  377.3 35.3 %collective-permute-start.61 = (f32[4,642]{1,0:T(4,128)}, f32[4,642]{1,0:T(4,128)S(1)}, u32[]{:S(2)}, u32[]{:S(2)}) collective-permute-start(f32[4,642]{1,0:T(4,128)} %collective-permute-done.60), channel_id=1, source_target_pairs={{0,15},{1,0},{2,1},{3,2},{4,3},{5,4},{6,5},{7,6},{8,7},{9,8},{10,9... | collective-permute-start | bytes 30824 | tf_op jit(solution)/shard_map/ppermute | solution.py:21
  384.9 36.6 %collective-permute-start.64 = (f32[4,642]{1,0:T(4,128)}, f32[4,642]{1,0:T(4,128)S(1)}, u32[]{:S(2)}, u32[]{:S(2)}) collective-permute-start(f32[4,642]{1,0:T(4,128)} %collective-permute-done.63), channel_id=1, source_target_pairs={{0,1},{1,2},{2,3},{3,4},{4,5},{5,6},{6,7},{7,8},{8,9},{9,10},{10,1... | collective-permute-start | bytes 30824 | tf_op jit(solution)/shard_map/ppermute | solution.py:21
  386.8 36.6 %collective-permute-start.68 = (f32[4,642]{1,0:T(4,128)}, f32[4,642]{1,0:T(4,128)S(1)}, u32[]{:S(2)}, u32[]{:S(2)}) collective-permute-start(f32[4,642]{1,0:T(4,128)} %collective-permute-done.67), channel_id=1, source_target_pairs={{0,15},{1,0},{2,1},{3,2},{4,3},{5,4},{6,5},{7,6},{8,7},{9,8},{10,9... | collective-permute-start | bytes 30824 | tf_op jit(solution)/shard_map/ppermute | solution.py:21
  394.1 36.6 %collective-permute-start.71 = (f32[4,642]{1,0:T(4,128)}, f32[4,642]{1,0:T(4,128)S(1)}, u32[]{:S(2)}, u32[]{:S(2)}) collective-permute-start(f32[4,642]{1,0:T(4,128)} %collective-permute-done.70), channel_id=1, source_target_pairs={{0,1},{1,2},{2,3},{3,4},{4,5},{5,6},{6,7},{7,8},{8,9},{9,10},{10,1... | collective-permute-start | bytes 30824 | tf_op jit(solution)/shard_map/ppermute | solution.py:21
  396.1 38.3 %collective-permute-start.48 = (f32[4,3,642]{2,1,0:T(4,128)S(1)}, f32[4,3,642]{2,1,0:T(4,128)S(1)}, u32[]{:S(2)}, u32[]{:S(2)}) collective-permute-start(f32[4,3,642]{2,1,0:T(4,128)S(1)} %gather_fusion.9), channel_id=1, source_target_pairs={{0,496},{16,0},{32,16},{48,32},{64,48},{80,64},{96,80},{112,96},{1... | collective-permute-start | bytes 92456 | tf_op jit(solution)/shard_map/ppermute | solution.py:21
  412.6 36.6 %collective-permute-start.50 = (f32[4,3,642]{2,1,0:T(4,128)}, f32[4,3,642]{2,1,0:T(4,128)}, u32[]{:S(2)}, u32[]{:S(2)}) collective-permute-start(f32[4,3,642]{2,1,0:T(4,128)} %gather_fusion.10), channel_id=1, source_target_pairs={{0,496},{16,0},{32,16},{48,32},{64,48},{80,64},{96,80},{112,96},{1... | collective-permute-start | bytes 92456 | tf_op jit(solution)/shard_map/ppermute | solution.py:21
  421.5 29.7 %collective-permute-start.51 = (f32[4,3,642]{2,1,0:T(4,128)}, f32[4,3,642]{2,1,0:T(4,128)}, u32[]{:S(2)}, u32[]{:S(2)}) collective-permute-start(f32[4,3,642]{2,1,0:T(4,128)} %gather_fusion.11), channel_id=1, source_target_pairs={{0,496},{16,0},{32,16},{48,32},{64,48},{80,64},{96,80},{112,96},{1... | collective-permute-start | bytes 92456 | tf_op jit(solution)/shard_map/ppermute | solution.py:21
  423.4 42.3 %collective-permute-start.53 = (f32[4,3,642]{2,1,0:T(4,128)S(1)}, f32[4,3,642]{2,1,0:T(4,128)}, u32[]{:S(2)}, u32[]{:S(2)}) collective-permute-start(f32[4,3,642]{2,1,0:T(4,128)S(1)} %gather_fusion.12), channel_id=1, source_target_pairs={{0,15},{1,0},{2,1},{3,2},{4,3},{5,4},{6,5},{7,6},{8,7},{9,8},{10,9... | collective-permute-start | bytes 92456 | tf_op jit(solution)/shard_map/ppermute | solution.py:21
  430.7 35.9 %collective-permute-start.54 = (f32[4,3,642]{2,1,0:T(4,128)S(1)}, f32[4,3,642]{2,1,0:T(4,128)}, u32[]{:S(2)}, u32[]{:S(2)}) collective-permute-start(f32[4,3,642]{2,1,0:T(4,128)S(1)} %gather_fusion.13), channel_id=1, source_target_pairs={{0,1},{1,2},{2,3},{3,4},{4,5},{5,6},{6,7},{7,8},{8,9},{9,10},{10,1... | collective-permute-start | bytes 92456 | tf_op jit(solution)/shard_map/ppermute | solution.py:21
  (92 other events, 1599.1 us)
where the time goes:
time: 480 us; the launch traced here: 477 us
  starting transfers between devices  289 us (60%)
  local copies, waits for them, and re-layouts  75.3 us (16%)
  waiting for transfers between devices  49.8 us (10%)
  matrix products  36.2 us (8%)
  other arithmetic  17.7 us (4%)
  between operations  8 us (2%)
    ppermute x72, starting transfers between devices, from_behind(): lax.ppermute(array, axis, [(i, (i + by) % size) for i in range(size)])  289 us
    ppermute x72, waiting for transfers between devices, from_behind(): lax.ppermute(array, axis, [(i, (i + by) % size) for i in range(size)])  49.8 us
    dot_general x10, matrix products, pair_forces(): cross = jnp.einsum('gca,gcv->gav', near_rows, far_rows, precision=highest)  16.2 us
    gather x8, local copies, waits for them, and re-layouts, per_device(): partner = cell_major[target_slots]  15.9 us
    unnamed x106, local copies, waits for them, and re-layouts  12.4 us
  transfers between devices with their start and end apart: 72, of which 14 were waited for; matrix products, arithmetic and copies ran while one was open for 26% of the time, Pallas kernels for 0%

commit v1 on v0

v1 whole, which is shorter than its diff:
```python
import functools

import jax
import jax.numpy as jnp
from jax import lax
from jax.experimental import pallas as pl
from jax.experimental.pallas import tpu as pltpu
from jax.sharding import PartitionSpec as P

V = 642
NBLK = 6
VB = 107
LANES = 128
CAP = 4
VPAD = 768
HEADINGS = 8

DIRECTIONS = ((-1, -1), (-1, 0), (-1, 1), (0, -1), (0, 1), (1, -1), (1, 0), (1, 1))
TENSION = 0.5
TIME_STEP = 0.25
FACTOR = 8.0 / VB
LOG2E = 1.4426950408889634
OFF = 1.0e6
MESH = pl.DeviceIdType.MESH
F32 = jnp.float32
BF16 = jnp.bfloat16


def mm(a, b):
    return lax.dot_general(a, b, (((1,), (0,)), ((), ())), preferred_element_type=F32)


def mm_nt(a, b):
    return lax.dot_general(a, b, (((1,), (1,)), ((), ())), preferred_element_type=F32)


def two_pieces(x):
    hi = x.astype(BF16)
    lo = (x - hi.astype(F32)).astype(BF16)
    return hi, lo


def three_pieces(x):
    hi = x.astype(BF16)
    rest = x - hi.astype(F32)
    mid = rest.astype(BF16)
    lo = (rest - mid.astype(F32)).astype(BF16)
    return hi, mid, lo


def id_table(ref):
    sub = lax.broadcasted_iota(jnp.int32, (8, LANES), 0) & 3
    tiles = []
    for h in range(HEADINGS):
        tile = jnp.where(
            sub == 0, ref[0, h], jnp.where(sub == 1, ref[1, h], jnp.where(sub == 2, ref[2, h], ref[3, h]))
        )
        tiles += [tile, tile]
    return jnp.concatenate(tiles, axis=0)


def kernel(
    n_gx, n_gy,
    x_hbm, met_hbm, cen_hbm, lap_hbm, bend_hbm, mig_s, ids_s, loc_s, cnt_s,
    off_o, met_o, cen_o,
    x, met, cen, lap, bend, wide, row_s, row_r, near_s, near_r, cell_s, cell_r,
    bt, qt, w, pp, disp, in_sem, send_sem, recv_sem,
):
    gx, gy = lax.axis_index("gx"), lax.axis_index("gy")

    def neighbour(h, sign):
        dx, dy = DIRECTIONS[h]
        return (
            lax.rem(gx + (sign * dx + n_gx), n_gx),
            lax.rem(gy + (sign * dy + n_gy), n_gy),
        )

    barrier = pltpu.get_barrier_semaphore()
    for h in range(HEADINGS):
        pl.semaphore_signal(barrier, inc=1, device_id=neighbour(h, 1), device_id_type=MESH)

    loads = [
        pltpu.make_async_copy(src, dst, in_sem.at[i])
        for i, (src, dst) in enumerate(
            ((x_hbm, x), (cen_hbm, cen), (met_hbm, met), (lap_hbm, lap), (bend_hbm, bend))
        )
    ]
    for load in loads:
        load.start()

    def send(kind, src, dst, h, sign):
        rows = pl.ds(16 * h, 16)
        return pltpu.make_async_remote_copy(
            src_ref=src.at[rows],
            dst_ref=dst.at[rows],
            send_sem=send_sem.at[kind, h],
            recv_sem=recv_sem.at[kind, h],
            device_id=neighbour(h, sign),
            device_id_type=MESH,
        )

    row = lax.broadcasted_iota(jnp.int32, (LANES, LANES), 0)
    lane = lax.broadcasted_iota(jnp.int32, (LANES, LANES), 1)
    rk = (row >> 2) & 3
    rj = row & 3

    def spread(one_hot, ks):
        return jnp.concatenate([jnp.where(rk == k, one_hot, 0.0) for k in ks], axis=1)

    ids = id_table(ids_s)
    owner = (ids * 10923) >> 16
    block = ids - NBLK * owner
    own_hot = (lane == owner).astype(F32)
    loc_hot = (lane == id_table(loc_s)).astype(F32)
    mig_hot = (lane == id_table(mig_s)).astype(F32)
    counts = jnp.concatenate(
        [jnp.full((16, LANES), cnt_s[0, h], jnp.int32) for h in range(HEADINGS)], axis=0
    )
    live = (rj < counts) & (lane < VB)

    loads[0].wait()
    loads[1].wait()
    x0, x1, x2 = x[0], x[1], x[2]
    xcat = jnp.concatenate([x0, x1, x2], axis=1)
    cen_rows = jnp.where(rk == 0, cen[0:1, :], jnp.where(rk == 1, cen[1:2, :], cen[2:3, :]))
    cen_rows = jnp.where(rk == 3, 0.0, cen_rows)
    wide[:, VPAD - LANES:] = jnp.zeros((LANES, LANES), F32)
    wide[:, :V] = mm_nt(spread(own_hot, (0, 1, 2)).astype(BF16), xcat)
    picked = jnp.zeros((LANES, LANES), F32)
    for b in range(NBLK):
        tile, shift = divmod(VB * b, LANES)
        two = wide[:, tile * LANES:(tile + 2) * LANES]
        if shift:
            two = pltpu.roll(two, 2 * LANES - shift, 1)
        picked = jnp.where(block == b, two[:, :LANES], picked)
    own_cen = jnp.sum(own_hot * cen_rows, axis=1, keepdims=True)
    row_s[...] = jnp.where(live, jnp.where(rk == 3, 1.0, picked + own_cen), 0.0)

    pl.semaphore_wait(barrier, HEADINGS)
    row_sends = [send(0, row_s, row_r, h, 1) for h in range(HEADINGS)]
    for copy in row_sends:
        copy.start()

    loc_spread = spread(loc_hot, (0, 1, 2)).astype(BF16)
    f0, f1, f2 = x0.astype(F32), x1.astype(F32), x2.astype(F32)
    sq = (f0 * f0 + f1 * f1 + f2 * f2) * (-0.25 * LOG2E)
    source = jnp.concatenate([x0, x1, x2, *three_pieces(sq)], axis=1)
    none = jnp.zeros((LANES, 3 * LANES), BF16)
    take_q = jnp.concatenate([loc_spread, none], axis=1)
    take_sq = jnp.concatenate([none, loc_spread], axis=1)
    parts = []
    for h in range(HEADINGS):
        rows = slice(16 * h, 16 * h + 16)
        parts += [take_q[rows], take_q[rows], take_q[rows], take_sq[rows]]
    take = jnp.concatenate(parts, axis=0)
    col = lax.broadcasted_iota(jnp.int32, (1, 512), 1)
    ones_col = jnp.where((((col >> 4) & 3) < 3) & (((col >> 2) & 3) == 3), 1.0, 0.0)
    bt[...] = (mm_nt(source, take) + ones_col).astype(BF16)
    ones_row = jnp.where(rk == 3, 1.0, 0.0)[:, :1]
    qt[...] = (mm_nt(loc_spread, xcat) + ones_row).astype(BF16)
    loc_cen = jnp.sum(loc_hot * cen_rows, axis=1, keepdims=True)

    loads[2].wait()
    loads[3].wait()
    loads[4].wait()
    metric = met[...]
    m1 = metric.astype(F32)
    m3 = jnp.concatenate([m1, m1, m1], axis=1)
    curvature = mm(lap[...], xcat)
    weighted = (m3 * curvature).astype(BF16)
    force = m3 * (TENSION * curvature - mm(lap[...], weighted)) - mm(bend[...], xcat)
    cen3 = jnp.concatenate([cen[0:1, :], cen[1:2, :], cen[2:3, :]], axis=1)
    xf = jnp.concatenate([f0, f1, f2], axis=1)
    disp[...] = xf + cen3 + TIME_STEP * force

    for copy in row_sends:
        copy.wait()

    got = row_r[...]
    rel = got - loc_cen
    rel_sq = jnp.where(rk == 3, 0.0, rel * rel)
    tot = pltpu.roll(rel_sq, 4, 0) + pltpu.roll(rel_sq, 8, 0) + pltpu.roll(rel_sq, 12, 0)
    vals = jnp.where(
        rk == 3, (-0.25 * LOG2E) * tot - OFF * (1.0 - got), (0.5 * LOG2E) * rel
    )
    v0, v1, v2 = three_pieces(vals)
    one16 = jnp.ones((16, LANES), BF16)
    near_sends = []
    for t in range(4):
        blocks = []
        for h in (2 * t, 2 * t + 1):
            rows = slice(16 * h, 16 * h + 16)
            blocks += [v0[rows], v1[rows], v2[rows], one16]
        base = jnp.concatenate(blocks, axis=0)
        left = bt[:, t * LANES:(t + 1) * LANES]
        for q in range(4):
            right = jnp.concatenate(
                [
                    jnp.where(((row >> 6) == (q // 2)) & (rj == 2 * (q % 2) + i), base, jnp.zeros_like(base))
                    for i in range(2)
                ],
                axis=1,
            )
            at = (t * 4 + q) * 256
            w[:, at:at + 256] = jnp.exp2(mm(left, right)).astype(BF16)
        rj16 = lax.broadcasted_iota(jnp.int32, (16, LANES), 0) & 3
        sums = []
        for h in (2 * t, 2 * t + 1):
            all4 = mm(qt[16 * h:16 * h + 16, :], w[:, 512 * h:512 * h + 512])
            mine = all4[:, :LANES]
            for j in range(1, 4):
                mine = jnp.where(rj16 == j, all4[:, j * LANES:(j + 1) * LANES], mine)
            sums.append(mine)
        total = jnp.concatenate(sums, axis=0)
        rk32 = rk[:32]
        weight = jnp.where(
            rk32 == 0,
            pltpu.roll(total, 20, 0),
            jnp.where(rk32 == 1, pltpu.roll(total, 24, 0), pltpu.roll(total, 28, 0)),
        )
        rows = slice(32 * t, 32 * t + 32)
        near_s[rows, :] = FACTOR * (rel[rows] * weight - total)
        for h in (2 * t, 2 * t + 1):
            copy = send(1, near_s, near_r, h, -1)
            copy.start()
            near_sends.append(copy)

    rel_t = jnp.transpose(jnp.where(rk == 3, 1.0, rel))
    rel_hi, rel_lo = two_pieces(rel_t)
    rel2 = jnp.concatenate([rel_hi, rel_lo], axis=1)
    lane2 = lax.broadcasted_iota(jnp.int32, (LANES, 2 * LANES), 1) & 127
    for h in range(HEADINGS):
        for j in range(CAP):
            at = (4 * h + j) * LANES
            pp[at:at + LANES, :] = jnp.where(
                ((lane2 >> 4) == h) & ((lane2 & 3) == j), rel2, jnp.zeros_like(rel2)
            )
    far2 = mm(w[...], pp[...])
    far = jnp.concatenate(two_pieces(far2[:, :LANES] + far2[:, LANES:]), axis=1)
    loc_put = spread(loc_hot, (0, 1, 2, 3)).astype(BF16)
    put = mm(far, jnp.concatenate([loc_put, loc_put], axis=0))
    put3 = put[:, 3 * LANES:]
    weight3 = jnp.concatenate([put3, put3, put3], axis=1)
    disp[...] = disp[...] - (TIME_STEP * FACTOR) * (put[:, :3 * LANES] - xf * weight3)

    own_spread = spread(own_hot, (0, 1, 2))
    block3 = jnp.concatenate([block, block, block], axis=1)
    near_put = jnp.concatenate(
        [jnp.where(block3 == b, own_spread, 0.0).astype(BF16) for b in range(NBLK)], axis=1
    )
    near_put = jnp.concatenate([near_put, near_put], axis=0)

    for copy in near_sends:
        copy.wait()
    near = jnp.concatenate(two_pieces(jnp.transpose(near_r[...])), axis=1)
    back = mm(near, near_put)
    for b in range(NBLK):
        rows = slice(VB * b, VB * b + VB)
        disp[rows, :] = disp[rows, :] + TIME_STEP * back[:VB, 384 * b:384 * b + 384]

    d_hi, d_lo = two_pieces(disp[...])
    moving = jnp.concatenate([d_hi, d_lo, metric], axis=1)
    pick3 = spread(mig_hot, (0, 1, 2))
    pick = jnp.concatenate([pick3, pick3, jnp.where(rk == 3, mig_hot, 0.0)], axis=1).astype(BF16)
    cell_s[:, VPAD - LANES:] = jnp.zeros((LANES, LANES), F32)
    cell_s[:, :V] = mm_nt(pick, moving)
    cell_sends = [send(2, cell_s, cell_r, h, 1) for h in range(HEADINGS)]
    for copy in cell_sends:
        copy.start()

    keep = 1.0 - jnp.sum(jnp.where(rk == 0, mig_hot, 0.0), axis=0, keepdims=True)
    keep3 = jnp.concatenate([keep, keep, keep], axis=1)
    mig_put = spread(mig_hot, (0, 1, 2, 3)).astype(BF16)
    mig_put = jnp.concatenate([mig_put, mig_put], axis=0)
    for copy in cell_sends:
        copy.wait()
    come = jnp.transpose(cell_r[...])[:V]
    arrived = mm(jnp.concatenate(two_pieces(come), axis=1), mig_put)
    met_o[...] = (m1 * keep + arrived[:, 3 * LANES:]).astype(BF16)
    settled = disp[...] * keep3 + arrived[:, :3 * LANES]
    centre = jnp.sum(settled, axis=0, keepdims=True) * (1.0 / V)
    offs = (settled - centre).astype(BF16)
    for k in range(3):
        off_o[k] = offs[:, k * LANES:(k + 1) * LANES]
        cen_o[k:k + 1, :] = centre[:, k * LANES:(k + 1) * LANES]


def solution(mesh):
    n_gx, n_gy = mesh.shape["gx"], mesh.shape["gy"]

    def per_device(offsets, metric, centers, lap, bend, mig_slots, contact_ids, contact_local, contact_count):
        hbm = pl.BlockSpec(memory_space=pl.ANY)
        smem = pl.BlockSpec(memory_space=pltpu.SMEM)
        vmem = pl.BlockSpec(memory_space=pltpu.VMEM)
        offs, met, cen = pl.pallas_call(
            functools.partial(kernel, n_gx, n_gy),
            out_shape=(
                jax.ShapeDtypeStruct((3, V, LANES), BF16),
                jax.ShapeDtypeStruct((V, LANES), BF16),
                jax.ShapeDtypeStruct((3, LANES), F32),
            ),
            in_specs=[hbm] * 5 + [smem] * 4,
            out_specs=(vmem, vmem, vmem),
            scratch_shapes=[
                pltpu.VMEM((3, V, LANES), BF16),
                pltpu.VMEM((V, LANES), BF16),
                pltpu.VMEM((3, LANES), F32),
                pltpu.VMEM((V, V), BF16),
                pltpu.VMEM((V, V), BF16),
                pltpu.VMEM((LANES, VPAD), F32),
                pltpu.VMEM((LANES, LANES), F32),
                pltpu.VMEM((LANES, LANES), F32),
                pltpu.VMEM((LANES, LANES), F32),
                pltpu.VMEM((LANES, LANES), F32),
                pltpu.VMEM((LANES, VPAD), F32),
                pltpu.VMEM((LANES, VPAD), F32),
                pltpu.VMEM((V, 512), BF16),
                pltpu.VMEM((LANES, V), BF16),
                pltpu.VMEM((V, 32 * LANES), BF16),
                pltpu.VMEM((32 * LANES, 2 * LANES), BF16),
                pltpu.VMEM((V, 3 * LANES), F32),
                pltpu.SemaphoreType.DMA((5,)),
                pltpu.SemaphoreType.DMA((3, HEADINGS)),
                pltpu.SemaphoreType.DMA((3, HEADINGS)),
            ],
            compiler_params=pltpu.CompilerParams(
                collective_id=0, has_side_effects=True, vmem_limit_bytes=56 * 1024 * 1024
            ),
        )(
            jnp.transpose(offsets, (1, 0, 2)),
            metric,
            centers,
            lap,
            bend,
            jnp.transpose(mig_slots[0]),
            jnp.transpose(contact_ids[0]),
            jnp.transpose(contact_local[0]),
            contact_count,
        )
        return jnp.transpose(offs, (1, 0, 2)), met, cen

    return jax.shard_map(
        per_device,
        mesh=mesh,
        in_specs=(
            P(None, None, ("gx", "gy")),
            P(None, ("gx", "gy")),
            P(None, ("gx", "gy")),
            P(),
            P(),
            P(("gx", "gy"), None, None),
            P(("gx", "gy"), None, None),
            P(("gx", "gy"), None, None),
            P(("gx", "gy"), None),
        ),
        out_specs=(P(None, None, ("gx", "gy")), P(None, ("gx", "gy")), P(None, ("gx", "gy"))),
        check_vma=False,
    )
```

time: 480 us -> 45.5 us (0.09)
  starting transfers between devices: 289 us -> 0 us
  local copies, waits for them, and re-layouts: 75.3 us -> 3.14 us
  waiting for transfers between devices: 49.8 us -> 0 us
  Pallas kernels: 0 us -> 41.5 us
  matrix products: 36.2 us -> 0 us
  other arithmetic: 17.7 us -> 0 us
  between operations: 8 us -> 0.65 us
    ppermute x72 -> x0, starting transfers between devices: 289 us -> none  [from_behind(): lax.ppermute(array, axis, [(i, (i + by) % size) for i in range(size)])]
    ppermute x72 -> x0, waiting for transfers between devices: 49.8 us -> none  [from_behind(): lax.ppermute(array, axis, [(i, (i + by) % size) for i in range(size)])]
    pallas_call x0 -> x1, Pallas kernels: none -> 41.5 us  [per_device(): pl.pallas_call(functools.partial(kernel, n_gx, n_gy), out_shape=(jax.Shap...]
    dot_general x33 -> x0, matrix products: 36.2 us -> none  [the longest x10 16.2 us: pair_forces(): cross = jnp.einsum('gca,gcv->gav', near_rows, far_rows, precision=highest)]
    gather x25 -> x0, local copies, waits for them, and re-layouts: 35.3 us -> none  [the longest x8 15.9 us: per_device(): partner = cell_major[target_slots]]
    reshape x6 -> x0, local copies, waits for them, and re-layouts: 11.3 us -> none  [the longest x2 3.91 us: per_device(): gridded = contact_major.reshape(cell_count, 3, NBLK, VB)]
    unnamed x106 -> x7, local copies, waits for them, and re-layouts: 12.4 us -> 3.14 us
    reduce_sum x29 -> x0, other arithmetic: 5.71 us -> none  [the longest x8 4.81 us: partner_work(): live_count = jnp.sum(active_in).astype(jnp.int32)]
  transfers between devices with their start and end apart: 72 -> 0, of which waited for: 14 -> 0; matrix products, arithmetic and copies ran while one was open for 26% -> 0% of each run, Pallas kernels for 0% -> 0%
where the time goes in v1:
time: 45.5 us; the launch traced here: 45.3 us
  Pallas kernels  41.5 us (91%)
  local copies, waits for them, and re-layouts  3.14 us (7%)
  between operations  0.65 us (1%)
    pallas_call x1, Pallas kernels, per_device(): pl.pallas_call(functools.partial(kernel, n_gx, n_gy), out_shape=(jax.Shap...  41.5 us
    unnamed x7, local copies, waits for them, and re-layouts  3.14 us

profile of v1, /device:TPU:1, one launch (start us, length us, event | category | flops | bytes accessed | tf_op | source)
XLA Modules:
  0.0 45.3 jit_solution(230816781324986706)
XLA Ops:
  0.6 41.5 %shard_map.112 = (bf16[3,642,128]{2,1,0:T(8,128)(2,1)}, bf16[642,128]{1,0:T(8,128)(2,1)}, f32[3,128]{1,0:T(4,128)}) custom-call(bf16[3,642,128]{2,1,0:T(8,128)(2,1)} %bitcast.11, bf16[642,128]{1,0:T(8,128)(2,1)} %met_hbm.1, f32[3,128]{1,0:T(4,128)} %cen_hbm.1, bf16[642,642]{1,0:T(8,128)(2,1)} %lap_hbm.1, bf16[642,642]{1,0:T(8,128)(2,1)} %bend_hbm.1, ...), custom_call_target="tpu_custom_call" | custom-call | tf_op jit(solution)/shard_map/pallas_call | solution.py:295
  42.2 0.0 copy-start
  42.2 1.9 %copy.15 = bf16[642,3,128]{2,0,1:T(8,128)(2,1)} copy(bf16[642,3,128]{2,0,1:T(8,128)(2,1)} %bitcast.12) | data formatting | bytes 986112
  44.1 0.0 copy-done
  44.1 0.0 copy-start.1
  44.1 0.7 %copy.16 = bf16[642,128]{1,0:T(8,128)(2,1)} copy(bf16[642,128]{1,0:T(8,128)(2,1)S(1)} %copy-done) | data formatting | bytes 328704
  44.7 0.0 copy-done.1
  44.7 0.6 %copy.17 = f32[3,128]{1,0:T(4,128)} copy(f32[3,128]{1,0:T(4,128)S(1)} %copy-done.1) | data formatting | bytes 3072
Async XLA Ops:
  42.2 1.9 %copy-start = (bf16[642,128]{1,0:T(8,128)(2,1)S(1)}, bf16[642,128]{1,0:T(8,128)(2,1)}, u32[]{:S(2)}) copy-start(bf16[642,128]{1,0:T(8,128)(2,1)} %get-tuple-element.13) | copy-start | bytes 493060
  44.1 0.7 %copy-start.1 = (f32[3,128]{1,0:T(4,128)S(1)}, f32[3,128]{1,0:T(4,128)}, u32[]{:S(2)}) copy-start(f32[3,128]{1,0:T(4,128)} %get-tuple-element.14) | copy-start | bytes 4612

commit v2 on v1

--- a/solution.py
+++ b/solution.py
@@ -13,6 +13,7 @@
 LANES = 128
 CAP = 4
 VPAD = 768
+HALF = 384
 HEADINGS = 8
 
 DIRECTIONS = ((-1, -1), (-1, 0), (-1, 1), (0, -1), (0, 1), (1, -1), (1, 0), (1, 1))
@@ -48,28 +49,29 @@
     return hi, mid, lo
 
 
-def id_table(ref):
+def id_table(ref, times):
     sub = lax.broadcasted_iota(jnp.int32, (8, LANES), 0) & 3
     tiles = []
     for h in range(HEADINGS):
         tile = jnp.where(
             sub == 0, ref[0, h], jnp.where(sub == 1, ref[1, h], jnp.where(sub == 2, ref[2, h], ref[3, h]))
         )
-        tiles += [tile, tile]
+        tiles += [tile] * times
     return jnp.concatenate(tiles, axis=0)
 
 
 def kernel(
     n_gx, n_gy,
     x_hbm, met_hbm, cen_hbm, lap_hbm, bend_hbm, mig_s, ids_s, loc_s, cnt_s,
-    off_o, met_o, cen_o,
-    x, met, cen, lap, bend, wide, row_s, row_r, near_s, near_r, cell_s, cell_r,
-    bt, qt, w, pp, disp, in_sem, send_sem, recv_sem,
+    stay_o, come_o, met_come_o, put_o, put_met_o,
+    x, met, cen, lap, bend, wide, row_s, row_r, near_s, near_r, cell_s, cell_r, wide2, met_out, met_in,
+    bt, qt, w, pp, disp, frame, rel_s, in_sem, send_sem, recv_sem,
 ):
     gx, gy = lax.axis_index("gx"), lax.axis_index("gy")
 
     def neighbour(h, sign):
-        dx, dy = DIRECTIONS[h]
+        nth = h + lax.div(h + 4, 8)
+        dx, dy = lax.div(nth, 3) - 1, lax.rem(nth, 3) - 1
         return (
             lax.rem(gx + (sign * dx + n_gx), n_gx),
             lax.rem(gy + (sign * dy + n_gy), n_gy),
@@ -88,8 +90,8 @@
     for load in loads:
         load.start()
 
-    def send(kind, src, dst, h, sign):
-        rows = pl.ds(16 * h, 16)
+    def send(kind, src, dst, h, sign, count=16):
+        rows = pl.ds(count * h, count)
         return pltpu.make_async_remote_copy(
             src_ref=src.at[rows],
             dst_ref=dst.at[rows],
@@ -107,12 +109,29 @@
     def spread(one_hot, ks):
         return jnp.concatenate([jnp.where(rk == k, one_hot, 0.0) for k in ks], axis=1)
 
-    ids = id_table(ids_s)
+    ids = id_table(ids_s, 2)
     owner = (ids * 10923) >> 16
     block = ids - NBLK * owner
     own_hot = (lane == owner).astype(F32)
-    loc_hot = (lane == id_table(loc_s)).astype(F32)
-    mig_hot = (lane == id_table(mig_s)).astype(F32)
+    loc_hot = (lane == id_table(loc_s, 2)).astype(F32)
+
+    def rows_lanes(rows):
+        shape = (rows, LANES)
+        return lax.broadcasted_iota(jnp.int32, shape, 0), lax.broadcasted_iota(jnp.int32, shape, 1)
+
+    row64, lane64 = rows_lanes(64)
+    row192, lane192 = rows_lanes(192)
+    late64 = (row64 & 4) == 4
+    late192 = (row192 & 4) == 4
+    tile192 = row192 >> 3
+    k192 = tile192 - 3 * ((tile192 * 171) >> 9)
+    met_hot = (lane64 == id_table(mig_s, 1)).astype(F32)
+    mig_hot = (lane192 == id_table(mig_s, 3)).astype(F32)
+
+    def halves(full, late):
+        late3 = jnp.concatenate([late, late, late], axis=1)
+        return jnp.where(late3, full[:, HALF:], full[:, :HALF])
+
     counts = jnp.concatenate(
         [jnp.full((16, LANES), cnt_s[0, h], jnp.int32) for h in range(HEADINGS)], axis=0
     )
@@ -141,6 +160,15 @@
     for copy in row_sends:
         copy.start()
 
+    loads[2].wait()
+    metric = met[...]
+    wide2[:, VPAD - LANES:] = jnp.zeros((192, LANES), F32)
+    wide2[:64, :V] = mm_nt(met_hot.astype(BF16), metric)
+    met_out[...] = halves(wide2[:64, :], late64)
+    metric_sends = [send(3, met_out, met_in, h, 1, 8) for h in range(HEADINGS)]
+    for copy in metric_sends:
+        copy.start()
+
     loc_spread = spread(loc_hot, (0, 1, 2)).astype(BF16)
     f0, f1, f2 = x0.astype(F32), x1.astype(F32), x2.astype(F32)
     sq = (f0 * f0 + f1 * f1 + f2 * f2) * (-0.25 * LOG2E)
@@ -158,12 +186,10 @@
     bt[...] = (mm_nt(source, take) + ones_col).astype(BF16)
     ones_row = jnp.where(rk == 3, 1.0, 0.0)[:, :1]
     qt[...] = (mm_nt(loc_spread, xcat) + ones_row).astype(BF16)
-    loc_cen = jnp.sum(loc_hot * cen_rows, axis=1, keepdims=True)
-
-    loads[2].wait()
+    frame[...] = jnp.broadcast_to(jnp.sum(loc_hot * cen_rows, axis=1, keepdims=True), (LANES, LANES))
+
     loads[3].wait()
     loads[4].wait()
-    metric = met[...]
     m1 = metric.astype(F32)
     m3 = jnp.concatenate([m1, m1, m1], axis=1)
     curvature = mm(lap[...], xcat)
@@ -173,26 +199,30 @@
     xf = jnp.concatenate([f0, f1, f2], axis=1)
     disp[...] = xf + cen3 + TIME_STEP * force
 
-    for copy in row_sends:
-        copy.wait()
-
-    got = row_r[...]
-    rel = got - loc_cen
-    rel_sq = jnp.where(rk == 3, 0.0, rel * rel)
-    tot = pltpu.roll(rel_sq, 4, 0) + pltpu.roll(rel_sq, 8, 0) + pltpu.roll(rel_sq, 12, 0)
-    vals = jnp.where(
-        rk == 3, (-0.25 * LOG2E) * tot - OFF * (1.0 - got), (0.5 * LOG2E) * rel
-    )
-    v0, v1, v2 = three_pieces(vals)
     one16 = jnp.ones((16, LANES), BF16)
+    row32, rk32 = row[:32], rk[:32]
+    rj16 = rj[:16]
+    backwards = lax.rem(gx + 1, n_gx // 2) == 0
     near_sends = []
-    for t in range(4):
-        blocks = []
-        for h in (2 * t, 2 * t + 1):
-            rows = slice(16 * h, 16 * h + 16)
-            blocks += [v0[rows], v1[rows], v2[rows], one16]
-        base = jnp.concatenate(blocks, axis=0)
-        left = bt[:, t * LANES:(t + 1) * LANES]
+    for step in range(4):
+        t = jnp.where(backwards, 3 - step, step)
+        for i in range(2):
+            send(0, row_s, row_r, 2 * t + i, 1).wait_recv()
+        rows = pl.ds(pl.multiple_of(32 * t, 32), 32)
+        got = row_r[rows, :]
+        rel = got - frame[rows, :]
+        rel_s[rows, :] = rel
+        rel_sq = jnp.where(rk32 == 3, 0.0, rel * rel)
+        tot = pltpu.roll(rel_sq, 4, 0) + pltpu.roll(rel_sq, 8, 0) + pltpu.roll(rel_sq, 12, 0)
+        vals = jnp.where(
+            rk32 == 3, (-0.25 * LOG2E) * tot - OFF * (1.0 - got), (0.5 * LOG2E) * rel
+        )
+        v0, v1, v2 = three_pieces(vals)
+        base = jnp.concatenate(
+            [v0[:16], v1[:16], v2[:16], one16, v0[16:], v1[16:], v2[16:], one16], axis=0
+        )
+        left = bt[:, pl.ds(pl.multiple_of(t * LANES, LANES), LANES)]
+        weights = []
         for q in range(4):
             right = jnp.concatenate(
                 [
@@ -201,31 +231,34 @@
                 ],
                 axis=1,
             )
-            at = (t * 4 + q) * 256
-            w[:, at:at + 256] = jnp.exp2(mm(left, right)).astype(BF16)
-        rj16 = lax.broadcasted_iota(jnp.int32, (16, LANES), 0) & 3
+            pair = jnp.exp2(mm(left, right)).astype(BF16)
+            w[:, pl.ds(pl.multiple_of(1024 * t + 256 * q, 256), 256)] = pair
+            weights.append(pair)
         sums = []
-        for h in (2 * t, 2 * t + 1):
-            all4 = mm(qt[16 * h:16 * h + 16, :], w[:, 512 * h:512 * h + 512])
-            mine = all4[:, :LANES]
-            for j in range(1, 4):
-                mine = jnp.where(rj16 == j, all4[:, j * LANES:(j + 1) * LANES], mine)
+        for i in range(2):
+            mine = None
+            partner = qt[pl.ds(pl.multiple_of(32 * t + 16 * i, 16), 16), :]
+            for j2 in range(2):
+                two = mm(partner, weights[2 * i + j2])
+                for j in range(2):
+                    part = two[:, j * LANES:(j + 1) * LANES]
+                    mine = part if mine is None else jnp.where(rj16 == 2 * j2 + j, part, mine)
             sums.append(mine)
         total = jnp.concatenate(sums, axis=0)
-        rk32 = rk[:32]
         weight = jnp.where(
             rk32 == 0,
             pltpu.roll(total, 20, 0),
             jnp.where(rk32 == 1, pltpu.roll(total, 24, 0), pltpu.roll(total, 28, 0)),
         )
-        rows = slice(32 * t, 32 * t + 32)
-        near_s[rows, :] = FACTOR * (rel[rows] * weight - total)
-        for h in (2 * t, 2 * t + 1):
-            copy = send(1, near_s, near_r, h, -1)
+        near_s[rows, :] = FACTOR * (rel * weight - total)
+        for i in range(2):
+            copy = send(1, near_s, near_r, 2 * t + i, -1)
             copy.start()
             near_sends.append(copy)
-
-    rel_t = jnp.transpose(jnp.where(rk == 3, 1.0, rel))
+    for copy in row_sends:
+        copy.wait_send()
+
+    rel_t = jnp.transpose(jnp.where(rk == 3, 1.0, rel_s[...]))
     rel_hi, rel_lo = two_pieces(rel_t)
     rel2 = jnp.concatenate([rel_hi, rel_lo], axis=1)
     lane2 = lax.broadcasted_iota(jnp.int32, (LANES, 2 * LANES), 1) & 127
@@ -243,7 +276,14 @@
     weight3 = jnp.concatenate([put3, put3, put3], axis=1)
     disp[...] = disp[...] - (TIME_STEP * FACTOR) * (put[:, :3 * LANES] - xf * weight3)
 
+    pick3 = jnp.concatenate([jnp.where(k192 == k, mig_hot, 0.0) for k in range(3)], axis=1).astype(BF16)
+    pick = jnp.concatenate([pick3, pick3], axis=1)
+    wide2[:, :V] = mm_nt(pick, jnp.concatenate(two_pieces(disp[...]), axis=1))
+    leave = halves(wide2[...], late192)
     own_spread = spread(own_hot, (0, 1, 2))
+    own_b16 = own_spread.astype(BF16)
+    same = (TIME_STEP * mm_nt(pick3, own_b16)).astype(BF16)
+    same = jnp.concatenate([same, same], axis=1)
     block3 = jnp.concatenate([block, block, block], axis=1)
     near_put = jnp.concatenate(
         [jnp.where(block3 == b, own_spread, 0.0).astype(BF16) for b in range(NBLK)], axis=1
@@ -252,32 +292,51 @@
 
     for copy in near_sends:
         copy.wait()
-    near = jnp.concatenate(two_pieces(jnp.transpose(near_r[...])), axis=1)
-    back = mm(near, near_put)
+    near = jnp.where(rk == 3, 0.0, near_r[...])
+    places = [jnp.zeros((LANES, LANES), F32) for _ in range(VPAD // LANES)]
+    for b in range(NBLK):
+        tile, shift = divmod(VB * b, LANES)
+        piece = jnp.where((block == b) & (lane < VB), near, 0.0)
+        if shift:
+            piece = pltpu.roll(piece, shift, 1)
+            places[tile + 1] = places[tile + 1] + jnp.where(lane < shift, piece, 0.0)
+            piece = jnp.where(lane >= shift, piece, 0.0)
+        places[tile] = places[tile] + piece
+    placed = jnp.concatenate(places, axis=1)
+    cell_s[...] = leave + halves(mm(same, jnp.concatenate(two_pieces(placed), axis=0)), late192)
+    cell_sends = [send(2, cell_s, cell_r, h, 1, 24) for h in range(HEADINGS)]
+    for copy in cell_sends:
+        copy.start()
+
+    near_t = jnp.concatenate(two_pieces(jnp.transpose(near)), axis=1)
+    back = mm(near_t, near_put)
     for b in range(NBLK):
         rows = slice(VB * b, VB * b + VB)
         disp[rows, :] = disp[rows, :] + TIME_STEP * back[:VB, 384 * b:384 * b + 384]
-
-    d_hi, d_lo = two_pieces(disp[...])
-    moving = jnp.concatenate([d_hi, d_lo, metric], axis=1)
-    pick3 = spread(mig_hot, (0, 1, 2))
-    pick = jnp.concatenate([pick3, pick3, jnp.where(rk == 3, mig_hot, 0.0)], axis=1).astype(BF16)
-    cell_s[:, VPAD - LANES:] = jnp.zeros((LANES, LANES), F32)
-    cell_s[:, :V] = mm_nt(pick, moving)
-    cell_sends = [send(2, cell_s, cell_r, h, 1) for h in range(HEADINGS)]
-    for copy in cell_sends:
-        copy.start()
-
-    keep = 1.0 - jnp.sum(jnp.where(rk == 0, mig_hot, 0.0), axis=0, keepdims=True)
+    keep = 1.0 - jnp.sum(jnp.where(late64, 0.0, met_hot), axis=0, keepdims=True)
     keep3 = jnp.concatenate([keep, keep, keep], axis=1)
-    mig_put = spread(mig_hot, (0, 1, 2, 3)).astype(BF16)
-    mig_put = jnp.concatenate([mig_put, mig_put], axis=0)
+    stay_o[:, :3 * LANES] = disp[...] * keep3
+    stay_o[:, 3 * LANES:] = m1 * keep
+    late3 = jnp.concatenate([late192, late192, late192], axis=1)
+    for half in range(2):
+        put = jnp.where(late3 == (half == 1), pick3, jnp.zeros_like(pick3))
+        put_o[half] = jnp.concatenate([put, put], axis=0)
+        put_met_o[half] = jnp.where(late64 == (half == 1), met_hot, 0.0).astype(BF16)
+    for copy in metric_sends:
+        copy.wait()
+    met_come_o[...] = met_in[...]
     for copy in cell_sends:
         copy.wait()
-    come = jnp.transpose(cell_r[...])[:V]
-    arrived = mm(jnp.concatenate(two_pieces(come), axis=1), mig_put)
-    met_o[...] = (m1 * keep + arrived[:, 3 * LANES:]).astype(BF16)
-    settled = disp[...] * keep3 + arrived[:, :3 * LANES]
+    come_o[...] = cell_r[...]
+
+
+def settle(stay, come, met_come, put, put_met, off_o, met_o, cen_o):
+    met_cells = jnp.transpose(met_come[...]).astype(BF16)
+    met_in = jnp.concatenate([mm(met_cells, put_met[0]), mm(met_cells, put_met[1])], axis=0)[:V]
+    met_o[...] = (stay[:, 3 * LANES:] + met_in).astype(BF16)
+    cells = jnp.concatenate(two_pieces(jnp.transpose(come[...])), axis=1)
+    arrived = jnp.concatenate([mm(cells, put[0]), mm(cells, put[1])], axis=0)[:V]
+    settled = stay[:, :3 * LANES] + arrived
     centre = jnp.sum(settled, axis=0, keepdims=True) * (1.0 / V)
     offs = (settled - centre).astype(BF16)
     for k in range(3):
@@ -289,18 +348,20 @@
     n_gx, n_gy = mesh.shape["gx"], mesh.shape["gy"]
 
     def per_device(offsets, metric, centers, lap, bend, mig_slots, contact_ids, contact_local, contact_count):
-        hbm = pl.BlockSpec(memory_space=pl.ANY)
+        hbm = pl.BlockSpec(memory_space=pltpu.HBM)
         smem = pl.BlockSpec(memory_space=pltpu.SMEM)
         vmem = pl.BlockSpec(memory_space=pltpu.VMEM)
-        offs, met, cen = pl.pallas_call(
+        parts = pl.pallas_call(
             functools.partial(kernel, n_gx, n_gy),
             out_shape=(
-                jax.ShapeDtypeStruct((3, V, LANES), BF16),
-                jax.ShapeDtypeStruct((V, LANES), BF16),
-                jax.ShapeDtypeStruct((3, LANES), F32),
+                pltpu.VMEM((V, 4 * LANES), F32),
+                pltpu.VMEM((192, HALF), F32),
+                pltpu.VMEM((64, HALF), F32),
+                pltpu.VMEM((2, HALF, 3 * LANES), BF16),
+                pltpu.VMEM((2, 64, LANES), BF16),
             ),
             in_specs=[hbm] * 5 + [smem] * 4,
-            out_specs=(vmem, vmem, vmem),
+            out_specs=(vmem,) * 5,
             scratch_shapes=[
                 pltpu.VMEM((3, V, LANES), BF16),
                 pltpu.VMEM((V, LANES), BF16),
@@ -312,19 +373,24 @@
                 pltpu.VMEM((LANES, LANES), F32),
                 pltpu.VMEM((LANES, LANES), F32),
                 pltpu.VMEM((LANES, LANES), F32),
-                pltpu.VMEM((LANES, VPAD), F32),
-                pltpu.VMEM((LANES, VPAD), F32),
+                pltpu.VMEM((192, HALF), F32),
+                pltpu.VMEM((192, HALF), F32),
+                pltpu.VMEM((192, VPAD), F32),
+                pltpu.VMEM((64, HALF), F32),
+                pltpu.VMEM((64, HALF), F32),
                 pltpu.VMEM((V, 512), BF16),
                 pltpu.VMEM((LANES, V), BF16),
                 pltpu.VMEM((V, 32 * LANES), BF16),
                 pltpu.VMEM((32 * LANES, 2 * LANES), BF16),
                 pltpu.VMEM((V, 3 * LANES), F32),
+                pltpu.VMEM((LANES, LANES), F32),
+                pltpu.VMEM((LANES, LANES), F32),
                 pltpu.SemaphoreType.DMA((5,)),
-                pltpu.SemaphoreType.DMA((3, HEADINGS)),
-                pltpu.SemaphoreType.DMA((3, HEADINGS)),
+                pltpu.SemaphoreType.DMA((4, HEADINGS)),
+                pltpu.SemaphoreType.DMA((4, HEADINGS)),
             ],
             compiler_params=pltpu.CompilerParams(
-                collective_id=0, has_side_effects=True, vmem_limit_bytes=56 * 1024 * 1024
+                collective_id=0, has_side_effects=True, vmem_limit_bytes=58 * 1024 * 1024
             ),
         )(
             jnp.transpose(offsets, (1, 0, 2)),
@@ -337,6 +403,17 @@
             jnp.transpose(contact_local[0]),
             contact_count,
         )
+        offs, met, cen = pl.pallas_call(
+            settle,
+            out_shape=(
+                jax.ShapeDtypeStruct((3, V, LANES), BF16),
+                jax.ShapeDtypeStruct((V, LANES), BF16),
+                jax.ShapeDtypeStruct((3, LANES), F32),
+            ),
+            in_specs=[vmem] * 5,
+            out_specs=(vmem, vmem, vmem),
+            compiler_params=pltpu.CompilerParams(vmem_limit_bytes=16 * 1024 * 1024),
+        )(*parts)
         return jnp.transpose(offs, (1, 0, 2)), met, cen
 
     return jax.shard_map(

time: 45.5 us -> 39 us (0.86)
  Pallas kernels: 41.5 us -> 38.2 us
  local copies, waits for them, and re-layouts: 3.14 us -> 0 us
    pallas_call x1 -> x2, Pallas kernels: 41.5 us -> 38.2 us  [the longest x1 36.4 us: per_device(): pl.pallas_call(functools.partial(kernel, n_gx, n_gy), out_shape=(pltpu.VM...]
    unnamed x7 -> x0, local copies, waits for them, and re-layouts: 3.14 us -> none
where the time goes in v2:
time: 39 us; the launch traced here: 38.8 us
  Pallas kernels  38.2 us (98%)
  between operations  0.64 us (2%)
    pallas_call x1, Pallas kernels, per_device(): pl.pallas_call(functools.partial(kernel, n_gx, n_gy), out_shape=(pltpu.VM...  36.4 us
    pallas_call x1, Pallas kernels, per_device(): pl.pallas_call(settle, out_shape=(jax.ShapeDtypeStruct((3, V, LANES), BF1...  1.79 us

profile of v2, /device:TPU:1, one launch (start us, length us, event | category | flops | bytes accessed | tf_op | source)
XLA Modules:
  0.0 38.8 jit_solution(6920058564338145918)
XLA Ops:
  0.6 36.4 %shard_map.112 = (f32[642,512]{1,0:T(8,128)S(1)}, f32[192,384]{1,0:T(8,128)S(1)}, f32[64,384]{1,0:T(8,128)S(1)}, bf16[2,384,384]{2,1,0:T(8,128)(2,1)S(1)}, bf16[2,64,128]{2,1,0:T(8,128)(2,1)S(1)}) custom-call(bf16[3,642,128]{2,1,0:T(8,128)(2,1)} %bitcast.11, bf16[642,128]{1,0:T(8,128)(2,1)} %met_hbm.1, f32[3,128]{1,0:T(4,128)} %cen_hbm.1, ...), custom_call_target="tpu_custom_call" | custom-call | tf_op jit(solution)/shard_map/pallas_call | solution.py:354
  37.1 1.8 %shard_map.113 = (bf16[3,642,128]{2,1,0:T(8,128)(2,1)}, bf16[642,128]{1,0:T(8,128)(2,1)}, f32[3,128]{1,0:T(4,128)}) custom-call(f32[642,512]{1,0:T(8,128)S(1)} %get-tuple-element.11.stay, f32[192,384]{1,0:T(8,128)S(1)} %get-tuple-element.12.come, f32[64,384]{1,0:T(8,128)S(1)} %get-tuple-element.13.met_come, bf16[2,384,384]{2,1,0:T(8,128)(2,1)S(1)} %get-tuple-element.14.put, ...), custom_call_target="tpu_custom_call" | custom-call | tf_op jit(solution)/shard_map/pallas_call | solution.py:406

commit v3 on v2

--- a/solution.py
+++ b/solution.py
@@ -62,10 +62,10 @@
 
 def kernel(
     n_gx, n_gy,
-    x_hbm, met_hbm, cen_hbm, lap_hbm, bend_hbm, mig_s, ids_s, loc_s, cnt_s,
+    x_hbm, met_hbm, cen_hbm, lap_hbm, bend_hbm, mig_hbm, ids_hbm, loc_hbm, cnt_hbm,
     stay_o, come_o, met_come_o, put_o, put_met_o,
     x, met, cen, lap, bend, wide, row_s, row_r, near_s, near_r, cell_s, cell_r, wide2, met_out, met_in,
-    bt, qt, w, pp, disp, frame, rel_s, in_sem, send_sem, recv_sem,
+    bt, qt, w, pp, disp, frame, rel_s, mig_s, ids_s, loc_s, cnt_s, in_sem, send_sem, recv_sem,
 ):
     gx, gy = lax.axis_index("gx"), lax.axis_index("gy")
 
@@ -84,10 +84,13 @@
     loads = [
         pltpu.make_async_copy(src, dst, in_sem.at[i])
         for i, (src, dst) in enumerate(
-            ((x_hbm, x), (cen_hbm, cen), (met_hbm, met), (lap_hbm, lap), (bend_hbm, bend))
+            (
+                (x_hbm, x), (cen_hbm, cen), (met_hbm, met), (lap_hbm, lap), (bend_hbm, bend),
+                (ids_hbm, ids_s), (cnt_hbm, cnt_s), (mig_hbm, mig_s), (loc_hbm, loc_s),
+            )
         )
     ]
-    for load in loads:
+    for load in loads[5:] + loads[:5]:
         load.start()
 
     def send(kind, src, dst, h, sign, count=16):
@@ -109,6 +112,8 @@
     def spread(one_hot, ks):
         return jnp.concatenate([jnp.where(rk == k, one_hot, 0.0) for k in ks], axis=1)
 
+    for load in loads[5:]:
+        load.wait()
     ids = id_table(ids_s, 2)
     owner = (ids * 10923) >> 16
     block = ids - NBLK * owner
@@ -330,18 +335,26 @@
     come_o[...] = cell_r[...]
 
 
-def settle(stay, come, met_come, put, put_met, off_o, met_o, cen_o):
+def settle(stay, come, met_come, put, put_met, off_hbm, met_hbm, cen_hbm, off, met, cen, sem):
     met_cells = jnp.transpose(met_come[...]).astype(BF16)
     met_in = jnp.concatenate([mm(met_cells, put_met[0]), mm(met_cells, put_met[1])], axis=0)[:V]
-    met_o[...] = (stay[:, 3 * LANES:] + met_in).astype(BF16)
+    met[...] = (stay[:, 3 * LANES:] + met_in).astype(BF16)
+    copies = [pltpu.make_async_copy(met, met_hbm, sem.at[0])]
+    copies[0].start()
     cells = jnp.concatenate(two_pieces(jnp.transpose(come[...])), axis=1)
-    arrived = jnp.concatenate([mm(cells, put[0]), mm(cells, put[1])], axis=0)[:V]
-    settled = stay[:, :3 * LANES] + arrived
-    centre = jnp.sum(settled, axis=0, keepdims=True) * (1.0 / V)
-    offs = (settled - centre).astype(BF16)
     for k in range(3):
-        off_o[k] = offs[:, k * LANES:(k + 1) * LANES]
-        cen_o[k:k + 1, :] = centre[:, k * LANES:(k + 1) * LANES]
+        lanes = slice(k * LANES, (k + 1) * LANES)
+        arrived = jnp.concatenate([mm(cells, put[0][:, lanes]), mm(cells, put[1][:, lanes])], axis=0)[:V]
+        settled = stay[:, lanes] + arrived
+        centre = jnp.sum(settled, axis=0, keepdims=True) * (1.0 / V)
+        off[k] = (settled - centre).astype(BF16)
+        cen[k:k + 1, :] = centre
+        copies.append(pltpu.make_async_copy(off.at[k], off_hbm.at[k], sem.at[k + 1]))
+        copies[-1].start()
+    copies.append(pltpu.make_async_copy(cen, cen_hbm, sem.at[4]))
+    copies[-1].start()
+    for copy in copies:
+        copy.wait()
 
 
 def solution(mesh):
@@ -349,7 +362,6 @@
 
     def per_device(offsets, metric, centers, lap, bend, mig_slots, contact_ids, contact_local, contact_count):
         hbm = pl.BlockSpec(memory_space=pltpu.HBM)
-        smem = pl.BlockSpec(memory_space=pltpu.SMEM)
         vmem = pl.BlockSpec(memory_space=pltpu.VMEM)
         parts = pl.pallas_call(
             functools.partial(kernel, n_gx, n_gy),
@@ -360,7 +372,7 @@
                 pltpu.VMEM((2, HALF, 3 * LANES), BF16),
                 pltpu.VMEM((2, 64, LANES), BF16),
             ),
-            in_specs=[hbm] * 5 + [smem] * 4,
+            in_specs=[hbm] * 9,
             out_specs=(vmem,) * 5,
             scratch_shapes=[
                 pltpu.VMEM((3, V, LANES), BF16),
@@ -385,7 +397,11 @@
                 pltpu.VMEM((V, 3 * LANES), F32),
                 pltpu.VMEM((LANES, LANES), F32),
                 pltpu.VMEM((LANES, LANES), F32),
-                pltpu.SemaphoreType.DMA((5,)),
+                pltpu.SMEM((CAP, HEADINGS), jnp.int32),
+                pltpu.SMEM((CAP, HEADINGS), jnp.int32),
+                pltpu.SMEM((CAP, HEADINGS), jnp.int32),
+                pltpu.SMEM((1, HEADINGS), jnp.int32),
+                pltpu.SemaphoreType.DMA((9,)),
                 pltpu.SemaphoreType.DMA((4, HEADINGS)),
                 pltpu.SemaphoreType.DMA((4, HEADINGS)),
             ],
@@ -411,7 +427,13 @@
                 jax.ShapeDtypeStruct((3, LANES), F32),
             ),
             in_specs=[vmem] * 5,
-            out_specs=(vmem, vmem, vmem),
+            out_specs=(hbm, hbm, hbm),
+            scratch_shapes=[
+                pltpu.VMEM((3, V, LANES), BF16),
+                pltpu.VMEM((V, LANES), BF16),
+                pltpu.VMEM((3, LANES), F32),
+                pltpu.SemaphoreType.DMA((5,)),
+            ],
             compiler_params=pltpu.CompilerParams(vmem_limit_bytes=16 * 1024 * 1024),
         )(*parts)
         return jnp.transpose(offs, (1, 0, 2)), met, cen

time: 39 us -> 38.1 us (0.977)
  Pallas kernels: 38.2 us -> 37.3 us
    pallas_call x1, Pallas kernels: 36.4 us -> 35.6 us  [per_device(): pl.pallas_call(functools.partial(kernel, n_gx, n_gy), out_shape=(pltpu.VM...]
where the time goes in v3:
time: 38.1 us; the launch traced here: 37.9 us
  Pallas kernels  37.3 us (98%)
  between operations  0.64 us (2%)
    pallas_call x1, Pallas kernels, per_device(): pl.pallas_call(functools.partial(kernel, n_gx, n_gy), out_shape=(pltpu.VM...  35.6 us
    pallas_call x1, Pallas kernels, per_device(): pl.pallas_call(settle, out_shape=(jax.ShapeDtypeStruct((3, V, LANES), BF1...  1.64 us

profile of v3, /device:TPU:1, one launch (start us, length us, event | category | flops | bytes accessed | tf_op | source)
XLA Modules:
  0.0 37.9 jit_solution(5645754579351382408)
XLA Ops:
  0.6 35.6 %shard_map.112 = (f32[642,512]{1,0:T(8,128)S(1)}, f32[192,384]{1,0:T(8,128)S(1)}, f32[64,384]{1,0:T(8,128)S(1)}, bf16[2,384,384]{2,1,0:T(8,128)(2,1)S(1)}, bf16[2,64,128]{2,1,0:T(8,128)(2,1)S(1)}) custom-call(bf16[3,642,128]{2,1,0:T(8,128)(2,1)} %bitcast.11, bf16[642,128]{1,0:T(8,128)(2,1)} %met_hbm.1, f32[3,128]{1,0:T(4,128)} %cen_hbm.1, ...), custom_call_target="tpu_custom_call" | custom-call | tf_op jit(solution)/shard_map/pallas_call | solution.py:366
  36.3 1.6 %shard_map.113 = (bf16[3,642,128]{2,1,0:T(8,128)(2,1)}, bf16[642,128]{1,0:T(8,128)(2,1)}, f32[3,128]{1,0:T(4,128)}) custom-call(f32[642,512]{1,0:T(8,128)S(1)} %get-tuple-element.11.stay, f32[192,384]{1,0:T(8,128)S(1)} %get-tuple-element.12.come, f32[64,384]{1,0:T(8,128)S(1)} %get-tuple-element.13.met_come, bf16[2,384,384]{2,1,0:T(8,128)(2,1)S(1)} %get-tuple-element.14.put, ...), custom_call_target="tpu_custom_call" | custom-call | tf_op jit(solution)/shard_map/pallas_call | solution.py:422

commit v4 on v3

--- a/solution.py
+++ b/solution.py
@@ -260,8 +260,6 @@
             copy = send(1, near_s, near_r, 2 * t + i, -1)
             copy.start()
             near_sends.append(copy)
-    for copy in row_sends:
-        copy.wait_send()
 
     rel_t = jnp.transpose(jnp.where(rk == 3, 1.0, rel_s[...]))
     rel_hi, rel_lo = two_pieces(rel_t)
@@ -296,7 +294,7 @@
     near_put = jnp.concatenate([near_put, near_put], axis=0)
 
     for copy in near_sends:
-        copy.wait()
+        copy.wait_recv()
     near = jnp.where(rk == 3, 0.0, near_r[...])
     places = [jnp.zeros((LANES, LANES), F32) for _ in range(VPAD // LANES)]
     for b in range(NBLK):
@@ -330,6 +328,8 @@
     for copy in metric_sends:
         copy.wait()
     met_come_o[...] = met_in[...]
+    for copy in row_sends + near_sends:
+        copy.wait_send()
     for copy in cell_sends:
         copy.wait()
     come_o[...] = cell_r[...]

time: 38.1 us -> 38.1 us (level)
  no operation moved by 1% of the time
where the time goes in v4:
time: 38.1 us; the launch traced here: 37.9 us
  Pallas kernels  37.3 us (98%)
  between operations  0.64 us (2%)
    pallas_call x1, Pallas kernels, per_device(): pl.pallas_call(functools.partial(kernel, n_gx, n_gy), out_shape=(pltpu.VM...  35.6 us
    pallas_call x1, Pallas kernels, per_device(): pl.pallas_call(settle, out_shape=(jax.ShapeDtypeStruct((3, V, LANES), BF1...  1.64 us

profile of v4, /device:TPU:1, one launch (start us, length us, event | category | flops | bytes accessed | tf_op | source)
XLA Modules:
  0.0 37.9 jit_solution(2000921021749013537)
XLA Ops:
  0.6 35.6 %shard_map.112 = (f32[642,512]{1,0:T(8,128)S(1)}, f32[192,384]{1,0:T(8,128)S(1)}, f32[64,384]{1,0:T(8,128)S(1)}, bf16[2,384,384]{2,1,0:T(8,128)(2,1)S(1)}, bf16[2,64,128]{2,1,0:T(8,128)(2,1)S(1)}) custom-call(bf16[3,642,128]{2,1,0:T(8,128)(2,1)} %bitcast.11, bf16[642,128]{1,0:T(8,128)(2,1)} %met_hbm.1, f32[3,128]{1,0:T(4,128)} %cen_hbm.1, ...), custom_call_target="tpu_custom_call" | custom-call | tf_op jit(solution)/shard_map/pallas_call | solution.py:366
  36.3 1.6 %shard_map.113 = (bf16[3,642,128]{2,1,0:T(8,128)(2,1)}, bf16[642,128]{1,0:T(8,128)(2,1)}, f32[3,128]{1,0:T(4,128)}) custom-call(f32[642,512]{1,0:T(8,128)S(1)} %get-tuple-element.11.stay, f32[192,384]{1,0:T(8,128)S(1)} %get-tuple-element.12.come, f32[64,384]{1,0:T(8,128)S(1)} %get-tuple-element.13.met_come, bf16[2,384,384]{2,1,0:T(8,128)(2,1)S(1)} %get-tuple-element.14.put, ...), custom_call_target="tpu_custom_call" | custom-call | tf_op jit(solution)/shard_map/pallas_call | solution.py:422
